TPU v7x, 32 devices: a whole 2x2x4 slice. The times are simulated.
32 devices in a mesh: vox: 8 (over y, x, core), chan: 4 (over z).
Axes of the slice: x: 2, y: 2, z: 4, core: 2. Of those that a mesh axis runs over, the one named last changes fastest.
Arguments:
- activations: bfloat16 [1024, 8, 512], P('chan', 'vox'), may hold values from -6 to 6
- upstream: bfloat16 [512, 8, 512], P('chan', 'vox'), may hold values from -6 to 6
- weights: bfloat16 [512, 27, 1024], P('chan'), may hold values from -0.0390625 to 0.0390625
Outputs:
- outputs: bfloat16 [512, 8, 512], P('chan', 'vox')
- input_grad: bfloat16 [1024, 8, 512], P('chan', 'vox')
- weight_grad: bfloat16 [512, 27, 1024], P('chan')
All inputs are finite; a program needn't handle non-finite values.
Results may differ from a plain program's by a relative error of at most 0.001.
Values may be sent and summed in bfloat16 or wider, within the bound.
A program may use at most 192 MiB of HBM per device.

v0:
```python
import jax
import jax.numpy as jnp
from jax import lax
from jax.sharding import PartitionSpec as P

NY = 32
NZ = 16


tap_offsets = [(a, b, c) for a in (-1, 0, 1) for b in (-1, 0, 1) for c in (-1, 0, 1)]


def padded_2(value, sides, width):
    for axis, dim in sides:
        size, length = (lax.axis_size(axis), value.shape[dim])
        up = [(i, (i + 1) % size) for i in range(size - 1)]
        down = [(j, i) for i, j in up]
        last = lax.slice_in_dim(value, length - width, length, axis=dim)
        leading = lax.slice_in_dim(value, 0, width, axis=dim)
        before = lax.ppermute(last, axis, up)
        after = lax.ppermute(leading, axis, down)
        value = jnp.concatenate([before, value, after], axis=dim)
    return value


def spread(slab_in, orient):
    channels = slab_in.shape[0]
    planes = slab_in.shape[1] - 2
    width = slab_in.shape[2]
    lane = lax.iota(jnp.int32, width) % NZ
    padded = jnp.pad(slab_in, ((0, 0), (0, 0), (NZ + 1, NZ + 1)))
    columns = []
    for offsets in tap_offsets:
        off_x = orient * offsets[0]
        off_y = orient * offsets[1]
        off_z = orient * offsets[2]
        start = NZ + 1 + off_y * NZ + off_z
        window = padded[:, 1 + off_x : 1 + off_x + planes, start : start + width]
        if off_z == -1:
            window = jnp.where(lane >= 1, window, jnp.zeros_like(window))
        elif off_z == 1:
            window = jnp.where(lane <= NZ - 2, window, jnp.zeros_like(window))
        columns.append(window.reshape(channels, planes * width))
    return jnp.stack(columns, axis=0)


def local(activations, upstream, weights):
    cin_dev = activations.shape[0]
    cout_dev = upstream.shape[0]
    slab_x = activations.shape[1]
    voxels = slab_x * NY * NZ
    x_halo = padded_2(activations, (("vox", 1),), 1)
    up_flat = upstream.reshape(cout_dev, voxels)
    panel = lax.all_gather(x_halo, "chan", axis=0, tiled=True)
    panel_rows = panel.shape[0]
    columns = spread(panel, 1).reshape(27 * panel_rows, voxels)
    w_panel = weights.reshape(cout_dev, 27 * panel_rows)
    out_total = jnp.dot(w_panel, columns, preferred_element_type=jnp.float32)
    grad_term = lax.dot_general(
        up_flat, columns, (((1,), (1,)), ((), ())), preferred_element_type=jnp.float32
    )
    grad_total = grad_term.reshape(cout_dev, 27, panel_rows)
    out_total, grad_local = (out_total, grad_total)
    outputs = out_total.reshape(cout_dev, slab_x, NY * NZ).astype(jnp.bfloat16)
    grad_scale = 1.0 / jnp.sqrt(jnp.float32(slab_x * lax.axis_size("vox") * NY * NZ))
    grad_whole = lax.psum(grad_local, "vox")
    weight_grad = (grad_whole * grad_scale).astype(jnp.bfloat16)
    dy_halo = padded_2(upstream, (("vox", 1),), 1)
    back_columns = spread(dy_halo, -1)
    partial_grad = jnp.einsum(
        "okc,kov->cv", weights, back_columns, preferred_element_type=jnp.float32
    )
    grad_sum = lax.psum_scatter(
        partial_grad.reshape(lax.axis_size("chan") * cin_dev, slab_x, NY * NZ),
        "chan",
        scatter_dimension=0,
        tiled=True,
    )
    input_grad = grad_sum.astype(jnp.bfloat16)
    return (outputs, input_grad, weight_grad)


def solution(mesh):
    return jax.shard_map(
        local,
        mesh=mesh,
        in_specs=(P("chan", "vox", None), P("chan", "vox", None), P("chan", None, None)),
        out_specs=(P("chan", "vox", None), P("chan", "vox", None), P("chan", None, None)),
        check_vma=False,
    )
```

profile of v0, /device:TPU:21, one launch (start us, length us, event | category | flops | bytes accessed | tf_op | source)
XLA Modules:
  0.0 405.7 jit_solution(16097379289238326183)
XLA Ops:
  7.2 1.1 copy.16
  8.3 2.6 collective-permute-start.1
  10.9 3.0 collective-permute-start
  13.9 1.0 copy.19
  14.9 1.9 collective-permute-start.3
  16.9 3.6 collective-permute-start.2
  21.2 1.5 collective-permute-done.2
  22.9 0.8 fusion.52
  26.6 0.8 fusion.45
  31.2 1.0 pad_maximum_fusion
  32.2 0.8 fusion.35
  44.3 8.3 %convolution_bitcast_fusion = f32[1024,1,512]{0,2,1:T(8,128)} fusion(bf16[27,128,512]{1,2,0:T(8,128)(2,1)} %fusion.12, bf16[128,27,1024]{2,0,1:T(8,128)(2,1)} %param.5), kind=kOutput, calls=%fused_computation.1 | convolution fusion | flops 3623878656 | bytes 12713984 | tf_op jit(solution)/shard_map/okc,kov->cv/dot_general | solution.py:70
  52.7 44.4 %all-gather.2.cloned.1.call-done = bf16[1024,3,512]{0,2,1:T(8,128)(2,1)} async-done(((bf16[256,3,512]{0,2,1:T(8,128)(2,1)}), bf16[1024,3,512]{0,2,1:T(8,128)(2,1)}) %all-gather.2.cloned.1.call-update) | async-done | bytes 3145744 | tf_op jit(solution)/shard_map/all_gather | solution.py:54
  97.1 2.7 bitcast_dynamic-update-slice_fusion.23
  99.7 1.1 bitcast_dynamic-update-slice_fusion.22
  100.8 1.3 bitcast_dynamic-update-slice_fusion.21
  102.1 1.4 bitcast_dynamic-update-slice_fusion.20
  103.5 1.0 fusion.4
  104.5 1.4 bitcast_dynamic-update-slice_fusion.19
  105.9 1.3 bitcast_dynamic-update-slice_fusion.18
  107.2 1.1 bitcast_dynamic-update-slice_fusion.17
  108.3 1.4 bitcast_dynamic-update-slice_fusion.16
  109.7 1.3 bitcast_dynamic-update-slice_fusion.15
  111.0 1.0 bitcast_dynamic-update-slice_fusion.14
  112.0 1.3 bitcast_dynamic-update-slice_fusion.13
  113.4 1.4 bitcast_dynamic-update-slice_fusion.12
  114.8 1.0 fusion.3
  115.8 1.3 bitcast_dynamic-update-slice_fusion.11
  117.2 1.3 bitcast_dynamic-update-slice_fusion.10
  118.5 1.0 bitcast_dynamic-update-slice_fusion.9
  119.5 1.4 bitcast_dynamic-update-slice_fusion.8
  120.9 1.3 bitcast_dynamic-update-slice_fusion.7
  122.2 1.1 bitcast_dynamic-update-slice_fusion.6
  123.3 1.3 bitcast_dynamic-update-slice_fusion.5
  124.6 1.4 bitcast_dynamic-update-slice_fusion.4
  126.0 1.1 fusion.2
  127.0 1.4 bitcast_dynamic-update-slice_fusion.3
  128.4 1.4 bitcast_dynamic-update-slice_fusion.2
  129.8 1.0 bitcast_dynamic-update-slice_fusion.1
  130.8 1.3 bitcast_dynamic-update-slice_fusion
  132.1 36.7 %copy.23 = bf16[27,1024,512]{2,1,0:T(8,128)(2,1)} copy(bf16[27,1024,512]{1,2,0:T(8,128)(2,1)} %bitcast_dynamic-update-slice_fusion) | data formatting | bytes 56623104 | tf_op jit(solution)/shard_map/stack | solution.py:44
  168.8 15.7 %fusion.53 = f32[27648,128]{1,0:T(8,128)} fusion(bf16[27648,512]{1,0:T(8,128)(2,1)} %bitcast.190, bf16[128,1,512]{2,0,1:T(8,128)(2,1)S(1)} %copy-done.1), kind=kOutput, calls=%fused_computation.110 | convolution fusion | flops 3623878656 | bytes 42598400 | tf_op jit(solution)/shard_map/dot_general | solution.py:59
  184.5 15.2 %copy.24 = f32[128,27,1024]{2,0,1:T(8,128)} copy(f32[128,27,1024]{0,2,1:T(8,128)} %bitcast.191) | data formatting | bytes 28311552 | tf_op jit(solution)/shard_map/reshape | solution.py:62
  199.8 1.1 convert_element_type.22
  200.8 0.8 copy.26
  201.7 16.4 %fusion.1 = bf16[128,1,512]{0,2,1:T(8,128)(2,1)S(1)} fusion(bf16[27,1024,512]{1,2,0:T(8,128)(2,1)} %bitcast_dynamic-update-slice_fusion, bf16[128,27,1024]{2,0,1:T(8,128)(2,1)} %param.5), kind=kOutput, calls=%fused_computation.6 | convolution fusion | flops 3623944192 | bytes 35520512 | tf_op jit(solution)/shard_map/dot_general | solution.py:58
  218.9 170.1 %all-reduce.4.cloned.1.call-done = f32[128,27,1024]{2,0,1:T(8,128)} async-done(((f32[128,27,1024]{2,0,1:T(8,128)}), f32[128,27,1024]{2,0,1:T(8,128)}) %all-reduce.4.cloned.1.call-update) | async-done | bytes 14155792 | tf_op jit(solution)/shard_map/psum | solution.py:66
  389.0 10.2 %multiply_convert_fusion = bf16[128,27,1024]{2,0,1:T(8,128)(2,1)} fusion(f32[128,27,1024]{2,0,1:T(8,128)} %all-reduce.4.cloned.1.call-done), kind=kLoop, calls=%fused_computation | loop fusion | flops 7077888 | bytes 21233664 | tf_op jit(solution)/shard_map/convert_element_type | solution.py:67
  (42 shorter events, 19.8 us)
Async XLA Ops:
  7.2 89.9 %all-gather.2.cloned.1.call-start = ((), (), s32[]{:S(2)}) async-start(), calls=%async_computation.1 | async-start | bytes 3932160 | tf_op jit(solution)/shard_map/all_gather | solution.py:54
  8.3 22.9 %collective-permute-start.1 = (bf16[256,1,512]{0,2,1:T(8,128)(2,1)S(1)}, bf16[256,1,512]{0,2,1:T(8,128)(2,1)S(1)}, u32[]{:S(2)}, u32[]{:S(2)}) collective-permute-start(bf16[256,1,512]{0,2,1:T(8,128)(2,1)S(1)} %copy.16), channel_id=1, source_target_pairs={{4,0},{8,4},{12,8},{16,12},{20,16},{24,20},{28,24},{5,1},{9,5},{13... | collective-permute-start | bytes 786440 | tf_op jit(solution)/shard_map/ppermute | solution.py:21
  10.9 20.3 %collective-permute-start = (bf16[256,1,512]{0,2,1:T(8,128)(2,1)S(1)}, bf16[256,1,512]{0,2,1:T(8,128)(2,1)S(1)}, u32[]{:S(2)}, u32[]{:S(2)}) collective-permute-start(bf16[256,1,512]{0,2,1:T(8,128)(2,1)S(1)} %copy.16), channel_id=1, source_target_pairs={{0,4},{4,8},{8,12},{12,16},{16,20},{20,24},{24,28},{1,5},{5,9},{9,... | collective-permute-start | bytes 786440 | tf_op jit(solution)/shard_map/ppermute | solution.py:20
  14.9 6.3 %collective-permute-start.3 = (bf16[128,1,512]{0,2,1:T(8,128)(2,1)S(1)}, bf16[128,1,512]{0,2,1:T(8,128)(2,1)S(1)}, u32[]{:S(2)}, u32[]{:S(2)}) collective-permute-start(bf16[128,1,512]{0,2,1:T(8,128)(2,1)S(1)} %copy.19), channel_id=1, source_target_pairs={{4,0},{8,4},{12,8},{16,12},{20,16},{24,20},{28,24},{5,1},{9,5},{13... | collective-permute-start | bytes 393224 | tf_op jit(solution)/shard_map/ppermute | solution.py:21
  16.9 5.9 %collective-permute-start.2 = (bf16[128,1,512]{0,2,1:T(8,128)(2,1)S(1)}, bf16[128,1,512]{0,2,1:T(8,128)(2,1)S(1)}, u32[]{:S(2)}, u32[]{:S(2)}) collective-permute-start(bf16[128,1,512]{0,2,1:T(8,128)(2,1)S(1)} %copy.19), channel_id=1, source_target_pairs={{0,4},{4,8},{8,12},{12,16},{16,20},{20,24},{24,28},{1,5},{5,9},{9,... | collective-permute-start | bytes 393224 | tf_op jit(solution)/shard_map/ppermute | solution.py:20
  32.1 167.6 %reduce-scatter.2.cloned.1.call-start = ((), (), s32[]{:S(2)}) async-start(), calls=%async_computation.2 | async-start | bytes 2621440 | tf_op jit(solution)/shard_map/reduce_scatter | solution.py:73
  52.7 336.4 %all-reduce.4.cloned.1.call-start = ((), (), s32[]{:S(2)}) async-start(), calls=%async_computation.3 | async-start | bytes 28311552 | tf_op jit(solution)/shard_map/psum | solution.py:66
  97.1 2.7 copy-start
  132.1 36.7 %copy-start.1 = (bf16[128,1,512]{2,0,1:T(8,128)(2,1)S(1)}, bf16[128,1,512]{2,0,1:T(8,128)(2,1)}, u32[]{:S(2)}) copy-start(bf16[128,1,512]{2,0,1:T(8,128)(2,1)} %param.4) | copy-start | bytes 393220
Sparse Core Ops, SparseCore 0:
  32.3 64.7 all-gather.1
  99.3 43.2 reduce-scatter.1
  199.9 189.1 all-reduce.3
where the time goes:
time: 409 us; the launch traced here: 406 us
  waiting for transfers between devices  217 us (53%)
  local copies, waits for them, and re-layouts  71.2 us (17%)
  other arithmetic  52.1 us (13%)
  matrix products  40.5 us (10%)
  between operations  13.9 us (3%)
  starting transfers between devices  11.3 us (3%)
    psum x1, waiting for transfers between devices, local(): grad_whole = lax.psum(grad_local, 'vox')  170 us
    all_gather x1, waiting for transfers between devices, local(): panel = lax.all_gather(x_halo, 'chan', axis=0, tiled=True)  44.4 us
    unnamed x34, other arithmetic  37.7 us
    another operation x1, local copies, waits for them, and re-layouts, spread(): return jnp.stack(columns, axis=0)  36.7 us
    unnamed x26, local copies, waits for them, and re-layouts  19.4 us
    dot_general x1, matrix products, local(): out_total = jnp.dot(w_panel, columns, preferred_element_type=jnp.float32)  16.4 us
    dot_general x1, matrix products, local(): lax.dot_general(up_flat, columns, (((1,), (1,)), ((), ())), preferred_ele...  15.7 us
    reshape x1, local copies, waits for them, and re-layouts, local(): grad_total = grad_term.reshape(cout_dev, 27, panel_rows)  15.2 us
  transfers between devices with their start and end apart: 7, of which 4 were waited for; matrix products, arithmetic and copies ran while one was open for 37% of the time, Pallas kernels for 0%

commit v1 on v0

v1 whole, which is shorter than its diff:
```python
import jax
import jax.numpy as jnp
from jax import lax
from jax.experimental import pallas as pl
from jax.experimental.pallas import tpu as pltpu
from jax.sharding import PartitionSpec as P

NY = 32
NZ = 16
PLANE = NY * NZ

in_plane = [(b, c) for b in (-1, 0, 1) for c in (-1, 0, 1)]


def moved(value, off_y, off_z):
    if off_y == 0 and off_z == 0:
        return value
    spot = lax.broadcasted_iota(jnp.int32, value.shape, 1)
    row, lane = spot // NZ + off_y, spot % NZ + off_z
    keep = (row >= 0) & (row < NY) & (lane >= 0) & (lane < NZ)
    turned = pltpu.roll(value, (-(off_y * NZ + off_z)) % PLANE, 1)
    return jnp.where(keep, turned, 0.0)


def back_kernel(up_ref, out_ref):
    for a in (-1, 0, 1):
        value = up_ref[1 - a].astype(jnp.float32)
        for t, (b, c) in enumerate(in_plane):
            out_ref[a + 1, t] = moved(value, -b, -c).astype(jnp.bfloat16)


def fold_kernel(z_ref, out_ref):
    total = jnp.zeros(out_ref.shape, jnp.float32)
    for t, (b, c) in enumerate(in_plane):
        total = total + moved(z_ref[t], b, c)
    out_ref[...] = total.astype(out_ref.dtype)


def wgrad_kernel(scale, up_ref, act_ref, out_ref, shifts, total):
    planes, rows = up_ref.shape[0], up_ref.shape[1]
    total[...] = jnp.zeros_like(total)

    @pl.loop(0, planes)
    def _(u):
        value = up_ref[u].astype(jnp.float32)
        for t, (b, c) in enumerate(in_plane):
            shifts[pl.ds(t * rows, rows), :] = moved(value, -b, -c).astype(jnp.bfloat16)
        for a in (-1, 0, 1):

            @pl.when((u + a >= 0) & (u + a < planes))
            def _():
                total[a + 1] += lax.dot_general(
                    shifts[...], act_ref[u + a], (((1,), (1,)), ((), ())), preferred_element_type=jnp.float32
                )

    for a in range(3):
        for t in range(9):
            out_ref[a * 9 + t] = (total[a, pl.ds(t * rows, rows), :] * scale).astype(jnp.bfloat16)


VMEM = pl.BlockSpec(memory_space=pltpu.VMEM)


def call(kernel, shape, dtype, flops, moved_bytes, limit, scratch=()):
    return pl.pallas_call(
        kernel,
        out_shape=jax.ShapeDtypeStruct(shape, dtype),
        out_specs=VMEM,
        scratch_shapes=list(scratch),
        compiler_params=pltpu.CompilerParams(vmem_limit_bytes=limit),
        cost_estimate=pl.CostEstimate(flops=flops, bytes_accessed=moved_bytes, transcendentals=0),
    )


def local(activations, upstream, weights):
    cin_dev = activations.shape[0]
    rows = upstream.shape[0]
    cin = weights.shape[2]
    vox, chan = lax.axis_size("vox"), lax.axis_size("chan")
    me = lax.axis_index("vox")
    half_id = me % 2
    half = cin // 2
    scale = (vox * activations.shape[1] * PLANE) ** -0.5
    pairs = [(i, i ^ 1) for i in range(vox)]
    act = activations.reshape(cin_dev, PLANE)
    up = upstream.reshape(rows, PLANE)

    panel = lax.all_gather(act, "chan", axis=0, tiled=True)
    up_all = lax.all_gather(up, "vox", axis=0, tiled=False)

    blank = jnp.zeros((1, rows, PLANE), jnp.bfloat16)
    up_near = lax.dynamic_slice_in_dim(jnp.concatenate([blank, up_all, blank]), me, 3, axis=0)
    back = call(back_kernel, (3, 9, rows, PLANE), jnp.bfloat16, 27 * rows * PLANE * 8, 30 * rows * PLANE * 2, 32 << 20)(up_near)
    part = jnp.einsum(
        "okc,kov->cv", weights, back.reshape(27, rows, PLANE), preferred_element_type=jnp.float32
    )
    input_grad = lax.psum_scatter(part, "chan", scatter_dimension=0, tiled=True)
    input_grad = input_grad.astype(jnp.bfloat16).reshape(cin_dev, 1, PLANE)

    other = lax.ppermute(lax.dynamic_slice_in_dim(panel, (1 - half_id) * half, half, axis=0), "vox", pairs)
    own = lax.dynamic_slice_in_dim(panel, half_id * half, half, axis=0)
    even = half_id == 0
    two = jnp.stack([jnp.where(even, own, other), jnp.where(even, other, own)])
    groups = [list(range(0, vox, 2)), list(range(1, vox, 2))]
    act_half = lax.all_gather(two, "vox", axis=0, tiled=True, axis_index_groups=groups)

    before = lax.ppermute(panel, "vox", [(i, i + 1) for i in range(vox - 1)])
    after = lax.ppermute(panel, "vox", [(i + 1, i) for i in range(vox - 1)])
    near = jnp.stack([before, panel, after])
    parts = jnp.einsum(
        "oabi,aip->bop", weights.reshape(rows, 3, 9, cin), near, preferred_element_type=jnp.float32
    )
    outputs = call(fold_kernel, (rows, PLANE), jnp.bfloat16, 9 * rows * PLANE * 8, 10 * rows * PLANE * 4, 32 << 20)(parts)
    outputs = outputs.reshape(rows, 1, PLANE)

    mine = call(
        lambda *refs: wgrad_kernel(scale, *refs),
        (27, rows, half),
        jnp.bfloat16,
        2 * 27 * rows * half * vox * PLANE,
        2 * (vox * PLANE * (rows + half) + 27 * rows * half),
        56 << 20,
        [pltpu.VMEM((9 * rows, PLANE), jnp.bfloat16), pltpu.VMEM((3, 9 * rows, half), jnp.float32)],
    )(up_all, act_half)
    theirs = lax.ppermute(mine, "vox", pairs)
    low, high = jnp.where(even, mine, theirs), jnp.where(even, theirs, mine)
    weight_grad = jnp.concatenate([low, high], axis=2).transpose(1, 0, 2)
    return outputs, input_grad, weight_grad


def solution(mesh):
    return jax.shard_map(
        local,
        mesh=mesh,
        in_specs=(P("chan", "vox", None), P("chan", "vox", None), P("chan", None, None)),
        out_specs=(P("chan", "vox", None), P("chan", "vox", None), P("chan", None, None)),
        check_vma=False,
    )
```

time: 409 us -> 202 us (0.49)
  waiting for transfers between devices: 217 us -> 119 us
  local copies, waits for them, and re-layouts: 71.2 us -> 4.34 us
  other arithmetic: 52.1 us -> 14.8 us
  Pallas kernels: 0 us -> 28.4 us
  matrix products: 40.5 us -> 13.9 us
  starting transfers between devices: 11.3 us -> 7.16 us
    psum x1 -> x0, waiting for transfers between devices: 170 us -> none  [local(): grad_whole = lax.psum(grad_local, 'vox')]
    all_gather x1 -> x3, waiting for transfers between devices: 44.4 us -> 95.5 us  [the longest x1 44.9 us: local(): lax.all_gather(two, 'vox', axis=0, tiled=True, axis_index_groups=groups)]
    unnamed x34 -> x0, other arithmetic: 37.7 us -> none
    another operation x1 -> x0, local copies, waits for them, and re-layouts: 36.7 us -> none  [spread(): return jnp.stack(columns, axis=0)]
    pallas_call x0 -> x3, Pallas kernels: none -> 28.4 us  [the longest x1 26 us: local(): call(lambda *refs: wgrad_kernel(scale, *refs), (27, rows, half), jnp.bflo...]
    dot_general x3 -> x2, matrix products: 40.5 us -> 13.9 us  [the longest x1 7.6 us: local(): jnp.einsum('okc,kov->cv', weights, back.reshape(27, rows, PLANE), preferr...]
    ppermute x4, waiting for transfers between devices: 2.2 us -> 22.4 us  [the longest x1 10.8 us: local(): after = lax.ppermute(panel, 'vox', [(i + 1, i) for i in range(vox - 1)])]
    unnamed x26 -> x4, local copies, waits for them, and re-layouts: 19.4 us -> 2.64 us
  transfers between devices with their start and end apart: 7 -> 8, of which waited for: 4 -> 6; matrix products, arithmetic and copies ran while one was open for 37% -> 10% of each run, Pallas kernels for 0% -> 14%
where the time goes in v1:
time: 202 us; the launch traced here: 201 us
  waiting for transfers between devices  119 us (59%)
  Pallas kernels  28.4 us (14%)
  other arithmetic  14.8 us (7%)
  matrix products  13.9 us (7%)
  between operations  13.9 us (7%)
  starting transfers between devices  7.16 us (4%)
  local copies, waits for them, and re-layouts  4.34 us (2%)
    all_gather x1, waiting for transfers between devices, local(): lax.all_gather(two, 'vox', axis=0, tiled=True, axis_index_groups=groups)  44.9 us
    all_gather x1, waiting for transfers between devices, local(): panel = lax.all_gather(act, 'chan', axis=0, tiled=True)  28.6 us
    pallas_call x1, Pallas kernels, local(): call(lambda *refs: wgrad_kernel(scale, *refs), (27, rows, half), jnp.bflo...  26 us
    all_gather x1, waiting for transfers between devices, local(): up_all = lax.all_gather(up, 'vox', axis=0, tiled=False)  22 us
    ppermute x1, waiting for transfers between devices, local(): after = lax.ppermute(panel, 'vox', [(i + 1, i) for i in range(vox - 1)])  10.8 us
    ppermute x1, waiting for transfers between devices, local(): before = lax.ppermute(panel, 'vox', [(i, i + 1) for i in range(vox - 1)])  10.2 us
    dot_general x1, matrix products, local(): jnp.einsum('okc,kov->cv', weights, back.reshape(27, rows, PLANE), preferr...  7.6 us
    dot_general x1, matrix products, local(): jnp.einsum('oabi,aip->bop', weights.reshape(rows, 3, 9, cin), near, prefe...  6.27 us
  transfers between devices with their start and end apart: 8, of which 6 were waited for; matrix products, arithmetic and copies ran while one was open for 10% of the time, Pallas kernels for 14%

profile of v1, /device:TPU:21, one launch (start us, length us, event | category | flops | bytes accessed | tf_op | source)
XLA Modules:
  0.0 201.1 jit_solution(16806206675722529800)
XLA Ops:
  7.2 0.0 all-gather.8.cloned.1.call-start
  7.2 1.8 copy.18
  9.0 0.0 all-gather.8.cloned.1.call-update
  9.0 0.0 all-gather.10.cloned.1.call-start
  9.1 0.7 all-gather.10.cloned.1.call-update
  9.8 0.0 all-gather.6.cloned.1.call-start
  9.8 28.6 %all-gather.8.cloned.1.call-done = bf16[1024,1,512]{0,2,1:T(8,128)(2,1)} async-done(((bf16[256,1,512]{0,2,1:T(8,128)(2,1)}), bf16[1024,1,512]{0,2,1:T(8,128)(2,1)}) %all-gather.8.cloned.1.call-update) | async-done | bytes 1048592 | tf_op jit(solution)/shard_map/all_gather | solution.py:88
  38.5 1.3 constant_dynamic-slice_fusion.1
  39.8 0.2 copy.23
  40.0 0.8 collective-permute-start.2
  40.8 0.2 copy.22
  41.0 1.3 collective-permute-done.2
  42.3 0.1 fusion.10
  42.4 1.1 pad_maximum_fusion
  43.4 0.0 all-gather.6.cloned.1.call-update
  43.5 0.0 reduce-scatter.2.cloned.1.call-start
  43.5 22.0 %all-gather.10.cloned.1.call-done = bf16[1024,1,512]{2,0,1:T(8,128)(2,1)} async-done(((bf16[128,1,512]{2,0,1:T(8,128)(2,1)}), bf16[1024,1,512]{2,0,1:T(8,128)(2,1)}) %all-gather.10.cloned.1.call-update) | async-done | bytes 1048592 | tf_op jit(solution)/shard_map/all_gather | solution.py:89
  65.5 1.2 fusion.13.up_ref
  66.6 1.0 shard_map.59
  67.7 7.6 %convolution_bitcast_fusion = f32[1024,512]{0,1:T(8,128)} fusion(bf16[27,128,512]{2,1,0:T(8,128)(2,1)S(1)} %bitcast.44, bf16[128,27,1024]{2,0,1:T(8,128)(2,1)} %param.5), kind=kOutput, calls=%fused_computation.11 | convolution fusion | flops 3623878656 | bytes 12713984 | tf_op jit(solution)/shard_map/okc,kov->cv/dot_general | solution.py:94
  75.3 0.0 reduce-scatter.2.cloned.1.call-update
  75.3 0.0 copy-start
  75.3 44.9 %all-gather.6.cloned.1.call-done.refs_1_ = bf16[8,512,512]{2,1,0:T(8,128)(2,1)} async-done(((bf16[2,512,512]{2,1,0:T(8,128)(2,1)}), bf16[8,512,512]{2,1,0:T(8,128)(2,1)}) %all-gather.6.cloned.1.call-update) | async-done | bytes 4194320 | tf_op jit(solution)/shard_map/all_gather | solution.py:105
  120.3 26.0 %shard_map.60 = bf16[27,128,512]{2,1,0:T(8,128)(2,1)} custom-call(bf16[8,128,512]{2,1,0:T(8,128)(2,1)} %bitcast.46, bf16[8,512,512]{2,1,0:T(8,128)(2,1)} %all-gather.6.cloned.1.call-done.refs_1_), custom_call_target="tpu_custom_call" | custom-call | flops 14495514624 | bytes 8781824 | tf_op jit(solution)/shard_map/pallas_call | solution.py:116
  146.3 0.7 collective-permute-start.3
  147.0 0.0 copy-done
  147.0 1.9 collective-permute-start.1
  148.9 3.6 %collective-permute-start = (bf16[1024,512]{0,1:T(8,128)(2,1)S(1)}, bf16[1024,512]{0,1:T(8,128)(2,1)S(1)}, u32[]{:S(2)}, u32[]{:S(2)}) collective-permute-start(bf16[1024,512]{0,1:T(8,128)(2,1)S(1)} %bitcast.48), channel_id=1, source_target_pairs={{0,4},{4,8},{8,12},{12,16},{16,20},{20,24},{24,28},{1,5},{5,9},{9,... | collective-permute-start | bytes 3145736 | tf_op jit(solution)/shard_map/ppermute | solution.py:107
  152.5 10.8 %collective-permute-done.1 = bf16[1024,512]{0,1:T(8,128)(2,1)S(1)} collective-permute-done((bf16[1024,512]{0,1:T(8,128)(2,1)S(1)}, bf16[1024,512]{0,1:T(8,128)(2,1)S(1)}, u32[]{:S(2)}, u32[]{:S(2)}) %collective-permute-start.1) | collective-permute-done | bytes 1048608 | tf_op jit(solution)/shard_map/ppermute | solution.py:108
  163.4 10.2 %collective-permute-done = bf16[1024,512]{0,1:T(8,128)(2,1)S(1)} collective-permute-done((bf16[1024,512]{0,1:T(8,128)(2,1)S(1)}, bf16[1024,512]{0,1:T(8,128)(2,1)S(1)}, u32[]{:S(2)}, u32[]{:S(2)}) %collective-permute-start) | collective-permute-done | bytes 1048608 | tf_op jit(solution)/shard_map/ppermute | solution.py:107
  173.6 6.3 %fusion.7.z_ref = f32[9,128,512]{2,1,0:T(8,128)S(1)} fusion(bf16[128,3,9,1024]{3,0,2,1:T(8,128)(2,1)} %bitcast.52, bf16[1,1024,512]{1,2,0:T(8,128)(2,1)S(1)} %bitcast.53, bf16[1,1024,512]{1,2,0:T(8,128)(2,1)S(1)} %bitcast.49, bf16[1,1024,512]{1,2,0:T(8,128)(2,1)S(1)} %bitcast.54), kind=kOutput, calls=%fused_computation.10 | convolution fusion | flops 3633315840 | bytes 12582912 | tf_op jit(solution)/shard_map/oabi,aip->bop/dot_general | solution.py:110
  179.9 1.3 shard_map.58
  181.2 0.0 reduce-scatter.2.cloned.1.call-done
  181.2 1.1 convert_bitcast_fusion
  182.3 0.8 copy.24
  183.1 0.0 collective-permute-done.3
  183.1 5.3 %broadcast_select_fusion.1 = (bf16[27,128,512]{2,1,0:T(8,128)(2,1)S(1)}, bf16[27,128,512]{2,1,0:T(8,128)(2,1)}) fusion(bf16[27,128,512]{2,1,0:T(8,128)(2,1)} %shard_map.60, bf16[27,128,512]{2,1,0:T(8,128)(2,1)} %collective-permute-done.3, pred[]{:T(512)S(6)} %eq.5), kind=kLoop, calls=%fused_computation.2 | loop fusion | flops 3538944 | bytes 14155777 | tf_op jit(solution)/shard_map/jit(_where)/select_n | solution.py:126
  188.4 6.1 %maximum_bitcast_fusion = bf16[128,27,1024]{2,0,1:T(8,128)(2,1)} fusion(bf16[27,128,512]{2,1,0:T(8,128)(2,1)} %get-tuple-element.13, bf16[27,128,512]{2,1,0:T(8,128)(2,1)S(1)} %get-tuple-element.12), kind=kLoop, calls=%fused_computation | loop fusion | flops 14155776 | bytes 14155776 | tf_op jit(solution)/shard_map/transpose | solution.py:127
  (1 shorter events, 0.0 us)
Async XLA Ops:
  7.2 31.3 %all-gather.8.cloned.1.call-start = ((), (), s32[]{:S(2)}) async-start(), calls=%async_computation.3 | async-start | bytes 1310720 | tf_op jit(solution)/shard_map/all_gather | solution.py:88
  9.0 56.4 %all-gather.10.cloned.1.call-start = ((), (), s32[]{:S(2)}) async-start(), calls=%async_computation.4 | async-start | bytes 1179648 | tf_op jit(solution)/shard_map/all_gather | solution.py:89
  9.8 110.5 %all-gather.6.cloned.1.call-start = ((), (), s32[]{:S(2)}) async-start(), calls=%async_computation.2 | async-start | bytes 5242880 | tf_op jit(solution)/shard_map/all_gather | solution.py:105
  40.0 2.3 %collective-permute-start.2 = (bf16[512,512]{1,0:T(8,128)(2,1)S(1)}, bf16[512,512]{1,0:T(8,128)(2,1)S(1)}, u32[]{:S(2)}, u32[]{:S(2)}) collective-permute-start(bf16[512,512]{1,0:T(8,128)(2,1)S(1)} %bitcast.50), channel_id=1, source_target_pairs={{0,4},{4,0},{8,12},{12,8},{16,20},{20,16},{24,28},{28,24},{1,5},{5... | collective-permute-start | bytes 1572872 | tf_op jit(solution)/shard_map/ppermute | solution.py:100
  43.5 137.7 %reduce-scatter.2.cloned.1.call-start = ((), (), s32[]{:S(2)}) async-start(), calls=%async_computation.1 | async-start | bytes 2621440 | tf_op jit(solution)/shard_map/reduce_scatter | solution.py:97
  75.3 71.7 %copy-start = (bf16[1024,1,512]{0,2,1:T(8,128)(2,1)S(1)}, bf16[1024,1,512]{0,2,1:T(8,128)(2,1)}, u32[]{:S(2)}) copy-start(bf16[1024,1,512]{0,2,1:T(8,128)(2,1)} %all-gather.8.cloned.1.call-done) | copy-start | bytes 3145732
  146.3 36.8 %collective-permute-start.3 = (bf16[27,128,512]{2,1,0:T(8,128)(2,1)}, bf16[27,128,512]{2,1,0:T(8,128)(2,1)}, u32[]{:S(2)}, u32[]{:S(2)}) collective-permute-start(bf16[27,128,512]{2,1,0:T(8,128)(2,1)} %shard_map.60), channel_id=1, source_target_pairs={{0,4},{4,0},{8,12},{12,8},{16,20},{20,16},{24,28},{28,24},{1,5},{5... | collective-permute-start | bytes 10616840 | tf_op jit(solution)/shard_map/ppermute | solution.py:125
  147.0 16.4 %collective-permute-start.1 = (bf16[1024,512]{0,1:T(8,128)(2,1)S(1)}, bf16[1024,512]{0,1:T(8,128)(2,1)S(1)}, u32[]{:S(2)}, u32[]{:S(2)}) collective-permute-start(bf16[1024,512]{0,1:T(8,128)(2,1)S(1)} %bitcast.47), channel_id=1, source_target_pairs={{4,0},{8,4},{12,8},{16,12},{20,16},{24,20},{28,24},{5,1},{9,5},{13... | collective-permute-start | bytes 3145736 | tf_op jit(solution)/shard_map/ppermute | solution.py:108
  148.9 24.7 %collective-permute-start = (bf16[1024,512]{0,1:T(8,128)(2,1)S(1)}, bf16[1024,512]{0,1:T(8,128)(2,1)S(1)}, u32[]{:S(2)}, u32[]{:S(2)}) collective-permute-start(bf16[1024,512]{0,1:T(8,128)(2,1)S(1)} %bitcast.48), channel_id=1, source_target_pairs={{0,4},{4,8},{8,12},{12,16},{16,20},{20,24},{24,28},{1,5},{5,9},{9,... | collective-permute-start | bytes 3145736 | tf_op jit(solution)/shard_map/ppermute | solution.py:107
Sparse Core Ops, SparseCore 0:
  10.1 28.3 all-gather.7
  40.4 25.0 all-gather.9
  67.9 52.3 all-gather.5
  122.4 43.2 reduce-scatter.1

commit v2 on v1

v2 whole, which is shorter than its diff:
```python
import jax
import jax.numpy as jnp
from jax import lax
from jax.experimental import pallas as pl
from jax.experimental.pallas import tpu as pltpu
from jax.sharding import PartitionSpec as P

NY = 32
NZ = 16
PLANE = NY * NZ

in_plane = [(b, c) for b in (-1, 0, 1) for c in (-1, 0, 1)]


def moved(value, off_y, off_z):
    if off_y == 0 and off_z == 0:
        return value
    spot = lax.broadcasted_iota(jnp.int32, value.shape, 1)
    row, lane = spot // NZ + off_y, spot % NZ + off_z
    keep = (row >= 0) & (row < NY) & (lane >= 0) & (lane < NZ)
    turned = pltpu.roll(value, (-(off_y * NZ + off_z)) % PLANE, 1)
    return jnp.where(keep, turned, 0.0)


def back_kernel(up_ref, out_ref):
    for a in (-1, 0, 1):
        value = up_ref[1 - a].astype(jnp.float32)
        for t, (b, c) in enumerate(in_plane):
            out_ref[a + 1, t] = moved(value, -b, -c).astype(jnp.bfloat16)


def fold_kernel(z_ref, out_ref):
    total = jnp.zeros(out_ref.shape, jnp.float32)
    for t, (b, c) in enumerate(in_plane):
        total = total + moved(z_ref[t], b, c)
    out_ref[...] = total.astype(out_ref.dtype)


def flipped(index, step, size):
    result, bit = 0, 1
    while bit < size:
        result = result + bit * ((index // bit + step // bit) % 2)
        bit *= 2
    return result


def wgrad_kernel(
    scale, vox, chan, act_ref, up_ref, out_ref, near_ref, pass_ref,
    panel, up_all, act_half, shifts, total,
    z_send, z_recv, up_send, up_recv, act_send, act_recv,
):
    me, z = lax.axis_index("vox"), lax.axis_index("chan")
    cin_dev, rows = act_ref.shape[0], up_ref.shape[0]
    side, spot = me % 2, me // 2
    blocks = chan // 2

    barrier = pltpu.get_barrier_semaphore()
    for d in range(1, chan):
        pl.semaphore_signal(barrier, inc=1, device_id=(me, flipped(z, d, chan)), device_id_type=pl.DeviceIdType.MESH)
    for d in range(1, vox):
        pl.semaphore_signal(barrier, inc=1, device_id=(flipped(me, d, vox), z), device_id_type=pl.DeviceIdType.MESH)
    pl.semaphore_wait(barrier, chan + vox - 2)

    def z_copy(d, source):
        return pltpu.make_async_remote_copy(
            src_ref=act_ref, dst_ref=panel.at[source], send_sem=z_send.at[d], recv_sem=z_recv.at[source],
            device_id=(me, flipped(z, d, chan)), device_id_type=pl.DeviceIdType.MESH,
        )

    def up_copy(d, source):
        return pltpu.make_async_remote_copy(
            src_ref=up_ref, dst_ref=up_all.at[source], send_sem=up_send.at[d], recv_sem=up_recv.at[source],
            device_id=(flipped(me, d, vox), z), device_id_type=pl.DeviceIdType.MESH,
        )

    def act_copy(block, d, source, target):
        place = block % blocks
        return pltpu.make_async_remote_copy(
            src_ref=panel.at[block],
            dst_ref=act_half.at[source, pl.ds(pl.multiple_of(place * cin_dev, cin_dev), cin_dev)],
            send_sem=act_send.at[block, d], recv_sem=act_recv.at[source, place],
            device_id=(target, z), device_id_type=pl.DeviceIdType.MESH,
        )

    def each_target(block, act):
        part = block // blocks
        for d in range(vox // 2):
            target = 2 * flipped(spot, d, vox // 2) + part
            if d == 0:

                @pl.when(part != side)
                def _():
                    act(act_copy(block, d, me, target))
            else:
                act(act_copy(block, d, me, target))

    for d in range(1, chan):
        z_copy(d, z).start()
    panel[z] = act_ref[...]
    each_target(z, lambda copy: copy.start())
    for d in range(1, vox):
        up_copy(d, me).start()
    up_all[me] = up_ref[...]
    total[...] = jnp.zeros_like(total)
    for d in range(1, chan):
        source = flipped(z, d, chan)
        z_copy(d, source).wait_recv()
        each_target(source, lambda copy: copy.start())

    @pl.loop(0, blocks)
    def _(place):
        at = pl.multiple_of(place * cin_dev, cin_dev)
        act_half[me, pl.ds(at, cin_dev), :] = panel[side * blocks + place]

    @pl.loop(0, vox)
    def _(d):
        u = flipped(me, d, vox)

        @pl.when(d > 0)
        def _():
            up_copy(d, u).wait_recv()

        value = up_all[u].astype(jnp.float32)
        for t, (b, c) in enumerate(in_plane):
            shifts[u, pl.ds(t * rows, rows), :] = moved(value, -b, -c).astype(jnp.bfloat16)

    @pl.loop(0, vox)
    def _(d):
        x = flipped(me, d, vox)

        @pl.when(d > 0)
        def _():
            for place in range(blocks):
                act_copy(place, 0, x, me).wait_recv()

        for a in (-1, 0, 1):

            @pl.when((x - a >= 0) & (x - a < vox))
            def _():
                total[a + 1] += lax.dot_general(
                    shifts[x - a], act_half[x], (((1,), (1,)), ((), ())), preferred_element_type=jnp.float32
                )

    for ref, centre in ((near_ref, me), (pass_ref, flipped(me, 1, vox))):
        for a in (-1, 0, 1):
            inside = (centre + a >= 0) & (centre + a < vox)

            @pl.when(inside)
            def _():
                ref[a + 1] = act_half[centre + a]

            @pl.when(jnp.logical_not(inside))
            def _():
                ref[a + 1] = jnp.zeros(ref.shape[1:], ref.dtype)

    for a in range(3):
        for t in range(9):
            out_ref[a * 9 + t] = (total[a, pl.ds(t * rows, rows), :] * scale).astype(jnp.bfloat16)

    for d in range(1, chan):
        z_copy(d, z).wait_send()
    for d in range(1, vox):
        up_copy(d, me).wait_send()
    for d in range(chan):
        each_target(flipped(z, d, chan), lambda copy: copy.wait_send())


def join_kernel(mine_ref, theirs_ref, out_ref, sems):
    half = mine_ref.shape[2]
    side = lax.axis_index("vox") % 2
    copies = [
        pltpu.make_async_copy(
            ref, out_ref.at[:, :, pl.ds(pl.multiple_of(place * half, half), half)], sems.at[n]
        )
        for n, (ref, place) in enumerate(((mine_ref, side), (theirs_ref, 1 - side)))
    ]
    for copy in copies:
        copy.start()
    for copy in copies:
        copy.wait()


VMEM = pl.BlockSpec(memory_space=pltpu.VMEM)


def call(kernel, shape, dtype, flops, moved_bytes, limit, scratch=()):
    return pl.pallas_call(
        kernel,
        out_shape=jax.ShapeDtypeStruct(shape, dtype),
        out_specs=VMEM,
        scratch_shapes=list(scratch),
        compiler_params=pltpu.CompilerParams(vmem_limit_bytes=limit),
        cost_estimate=pl.CostEstimate(flops=flops, bytes_accessed=moved_bytes, transcendentals=0),
    )


def local(activations, upstream, weights):
    cin_dev = activations.shape[0]
    rows = upstream.shape[0]
    cin = weights.shape[2]
    vox, chan = lax.axis_size("vox"), lax.axis_size("chan")
    even = lax.axis_index("vox") % 2 == 0
    half = cin // 2
    scale = (vox * activations.shape[1] * PLANE) ** -0.5
    pairs = [(i, i ^ 1) for i in range(vox)]
    act = activations.reshape(cin_dev, PLANE)
    up = upstream.reshape(rows, PLANE)

    below = lax.ppermute(up, "vox", [(i, i + 1) for i in range(vox - 1)])
    above = lax.ppermute(up, "vox", [(i + 1, i) for i in range(vox - 1)])
    up_near = jnp.stack([below, up, above])
    back = call(back_kernel, (3, 9, rows, PLANE), jnp.bfloat16, 27 * rows * PLANE * 8, 30 * rows * PLANE * 2, 32 << 20)(up_near)
    part = jnp.einsum(
        "okc,kov->cv", weights, back.reshape(27, rows, PLANE), preferred_element_type=jnp.float32
    )
    act, part = lax.optimization_barrier((act, part))
    input_grad = lax.psum_scatter(part, "chan", scatter_dimension=0, tiled=True)
    input_grad = input_grad.astype(jnp.bfloat16).reshape(cin_dev, 1, PLANE)

    dma = pltpu.SemaphoreType.DMA
    mine, near, passed = pl.pallas_call(
        lambda *refs: wgrad_kernel(scale, vox, chan, *refs),
        out_shape=(
            jax.ShapeDtypeStruct((27, rows, half), jnp.bfloat16),
            jax.ShapeDtypeStruct((3, half, PLANE), jnp.bfloat16),
            jax.ShapeDtypeStruct((3, half, PLANE), jnp.bfloat16),
        ),
        in_specs=[VMEM, VMEM],
        out_specs=(VMEM, VMEM, VMEM),
        scratch_shapes=[
            pltpu.VMEM((chan, cin_dev, PLANE), jnp.bfloat16),
            pltpu.VMEM((vox, rows, PLANE), jnp.bfloat16),
            pltpu.VMEM((vox, half, PLANE), jnp.bfloat16),
            pltpu.VMEM((vox, 9 * rows, PLANE), jnp.bfloat16),
            pltpu.VMEM((3, 9 * rows, half), jnp.float32),
            dma((chan,)),
            dma((chan,)),
            dma((vox,)),
            dma((vox,)),
            dma((chan, vox // 2)),
            dma((vox, chan // 2)),
        ],
        compiler_params=pltpu.CompilerParams(
            vmem_limit_bytes=56 << 20, collective_id=0, has_side_effects=True
        ),
        cost_estimate=pl.CostEstimate(
            flops=4 * 27 * rows * half * vox * PLANE,
            bytes_accessed=2 * (PLANE * (rows + cin_dev + 6 * half) + 27 * rows * half),
            transcendentals=0,
        ),
    )(act, up)

    rest = lax.ppermute(passed, "vox", pairs)
    theirs = lax.ppermute(mine, "vox", pairs)
    full = jnp.concatenate([jnp.where(even, near, rest), jnp.where(even, rest, near)], axis=1)
    parts = jnp.einsum(
        "oabi,aip->bop", weights.reshape(rows, 3, 9, cin), full, preferred_element_type=jnp.float32
    )
    outputs = call(fold_kernel, (rows, PLANE), jnp.bfloat16, 9 * rows * PLANE * 8, 10 * rows * PLANE * 4, 32 << 20)(parts)
    outputs = outputs.reshape(rows, 1, PLANE)

    anywhere = pl.BlockSpec(memory_space=pl.ANY)
    weight_grad = pl.pallas_call(
        join_kernel,
        out_shape=jax.ShapeDtypeStruct((27, rows, cin), jnp.bfloat16),
        in_specs=[anywhere, anywhere],
        out_specs=anywhere,
        scratch_shapes=[dma((2,))],
        cost_estimate=pl.CostEstimate(flops=0, bytes_accessed=4 * 27 * rows * cin, transcendentals=0),
    )(mine, theirs)
    return outputs, input_grad, weight_grad.transpose(1, 0, 2)


def solution(mesh):
    return jax.shard_map(
        local,
        mesh=mesh,
        in_specs=(P("chan", "vox", None), P("chan", "vox", None), P("chan", None, None)),
        out_specs=(P("chan", "vox", None), P("chan", "vox", None), P("chan", None, None)),
        check_vma=False,
    )
```

time: 202 us -> 349 us (1.73)
  Pallas kernels: 28.4 us -> 280 us
  waiting for transfers between devices: 119 us -> 10.5 us
  starting transfers between devices: 7.16 us -> 23.6 us
  other arithmetic: 14.8 us -> 4.11 us
    pallas_call x1 -> x2, Pallas kernels: 26 us -> 278 us  [the longest x1 216 us: local(): pl.pallas_call(join_kernel, out_shape=jax.ShapeDtypeStruct((27, rows, cin...]
    all_gather x3 -> x0, waiting for transfers between devices: 95.5 us -> none  [the longest x1 44.9 us: local(): lax.all_gather(two, 'vox', axis=0, tiled=True, axis_index_groups=groups)]
    ppermute x1, starting transfers between devices: 0.67 us -> 17.8 us  [local(): theirs = lax.ppermute(mine, 'vox', pairs)]
    ppermute x3, waiting for transfers between devices: 22.4 us -> 10.5 us  [the longest x1 8.23 us: local(): rest = lax.ppermute(passed, 'vox', pairs)]
    transpose x1 -> x0, other arithmetic: 6.13 us -> none  [local(): weight_grad = jnp.concatenate([low, high], axis=2).transpose(1, 0, 2)]
  transfers between devices with their start and end apart: 8 -> 5, of which waited for: 6 -> 3; matrix products, arithmetic and copies ran while one was open for 10% -> 2% of each run, Pallas kernels for 14% -> 80%
where the time goes in v2:
time: 349 us; the launch traced here: 348 us
  Pallas kernels  280 us (80%)
  starting transfers between devices  23.6 us (7%)
  between operations  14.1 us (4%)
  matrix products  13.6 us (4%)
  waiting for transfers between devices  10.5 us (3%)
  other arithmetic  4.11 us (1%)
    pallas_call x1, Pallas kernels, local(): pl.pallas_call(join_kernel, out_shape=jax.ShapeDtypeStruct((27, rows, cin...  216 us
    pallas_call x1, Pallas kernels, local(): pl.pallas_call(lambda *refs: wgrad_kernel(scale, vox, chan, *refs), out_s...  62 us
    ppermute x1, starting transfers between devices, local(): theirs = lax.ppermute(mine, 'vox', pairs)  17.8 us
    ppermute x1, waiting for transfers between devices, local(): rest = lax.ppermute(passed, 'vox', pairs)  8.23 us
    dot_general x1, matrix products, local(): jnp.einsum('okc,kov->cv', weights, back.reshape(27, rows, PLANE), preferr...  7.6 us
  transfers between devices with their start and end apart: 5, of which 3 were waited for; matrix products, arithmetic and copies ran while one was open for 2% of the time, Pallas kernels for 80%

profile of v2, /device:TPU:21, one launch (start us, length us, event | category | flops | bytes accessed | tf_op | source)
XLA Modules:
  0.0 348.5 jit_solution(11239828553345755347)
XLA Ops:
  7.2 0.0 reduce-scatter.2.cloned.1.call-start
  7.2 2.6 collective-permute-start.1
  9.8 3.0 collective-permute-start
  12.8 0.9 collective-permute-done.1
  13.7 1.3 collective-permute-done
  15.1 0.9 pad_maximum_fusion.up_ref
  16.0 1.0 shard_map.58
  17.1 7.6 %convolution_bitcast_fusion = f32[1024,512]{0,1:T(8,128)} fusion(bf16[27,128,512]{2,1,0:T(8,128)(2,1)S(1)} %bitcast.31, bf16[128,27,1024]{2,0,1:T(8,128)(2,1)} %param.5), kind=kOutput, calls=%fused_computation.6 | convolution fusion | flops 3623878656 | bytes 12713984 | tf_op jit(solution)/shard_map/okc,kov->cv/dot_general | solution.py:213
  24.7 0.0 reduce-scatter.2.cloned.1.call-update
  24.7 62.0 %shard_map.59 = (bf16[27,128,512]{2,1,0:T(8,128)(2,1)}, bf16[3,512,512]{2,1,0:T(8,128)(2,1)}, bf16[3,512,512]{2,1,0:T(8,128)(2,1)}) custom-call(bf16[256,512]{1,0:T(8,128)(2,1)} %bitcast.41, bf16[128,512]{1,0:T(8,128)(2,1)} %bitcast.37), custom_call_target="tpu_custom_call" | custom-call | flops 28991029248 | bytes 7077888 | tf_op jit(solution)/shard_map/pallas_call | solution.py:221
  86.7 17.8 %collective-permute-start.3 = (bf16[27,128,512]{2,1,0:T(8,128)(2,1)}, bf16[27,128,512]{2,1,0:T(8,128)(2,1)S(1)}, u32[]{:S(2)}, u32[]{:S(2)}) collective-permute-start(bf16[27,128,512]{2,1,0:T(8,128)(2,1)} %get-tuple-element.12.mine_ref), channel_id=1, source_target_pairs={{0,4},{4,0},{8,12},{12,8},{16,20},{20,16},{24,28},{28,24},{1,5},{5... | collective-permute-start | bytes 10616840 | tf_op jit(solution)/shard_map/ppermute | solution.py:254
  104.6 0.1 collective-permute-start.2
  104.6 8.2 %collective-permute-done.2 = bf16[3,512,512]{2,1,0:T(8,128)(2,1)} collective-permute-done((bf16[3,512,512]{2,1,0:T(8,128)(2,1)}, bf16[3,512,512]{2,1,0:T(8,128)(2,1)}, u32[]{:S(2)}, u32[]{:S(2)}) %collective-permute-start.2) | collective-permute-done | bytes 1572896 | tf_op jit(solution)/shard_map/ppermute | solution.py:253
  112.9 2.1 broadcast_select_fusion.1
  115.0 6.0 %fusion.5.z_ref = f32[9,128,512]{2,1,0:T(8,128)S(1)} fusion(bf16[128,3,9,1024]{3,0,2,1:T(8,128)(2,1)} %bitcast.40, bf16[3,512,512]{2,1,0:T(8,128)(2,1)S(1)} %get-tuple-element.17, bf16[3,512,512]{2,1,0:T(8,128)(2,1)S(1)} %get-tuple-element.16), kind=kOutput, calls=%fused_computation.5 | convolution fusion | flops 3630170112 | bytes 12582912 | tf_op jit(solution)/shard_map/oabi,aip->bop/dot_general | solution.py:256
  121.0 1.3 shard_map.60
  122.3 0.0 collective-permute-done.3.theirs_ref
  122.3 0.0 copy-start
  122.3 1.8 copy-done
  124.2 215.5 %shard_map.61 = bf16[27,128,1024]{2,1,0:T(8,128)(2,1)} custom-call(bf16[27,128,512]{2,1,0:T(8,128)(2,1)} %get-tuple-element.12.mine_ref, bf16[27,128,512]{2,1,0:T(8,128)(2,1)} %copy-done), custom_call_target="tpu_custom_call" | custom-call | bytes 14155776 | tf_op jit(solution)/shard_map/pallas_call | solution.py:263
  339.7 0.0 reduce-scatter.2.cloned.1.call-done
  339.7 1.1 convert_bitcast_fusion
  340.8 0.8 copy.10
Async XLA Ops:
  7.2 332.5 %reduce-scatter.2.cloned.1.call-start = ((), (), s32[]{:S(2)}) async-start(), calls=%async_computation.1 | async-start | bytes 2621440 | tf_op jit(solution)/shard_map/reduce_scatter | solution.py:217
  7.2 6.5 %collective-permute-start.1 = (bf16[128,512]{1,0:T(8,128)(2,1)}, bf16[128,512]{1,0:T(8,128)(2,1)S(1)}, u32[]{:S(2)}, u32[]{:S(2)}) collective-permute-start(bf16[128,512]{1,0:T(8,128)(2,1)} %bitcast.34), channel_id=1, source_target_pairs={{4,0},{8,4},{12,8},{16,12},{20,16},{24,20},{28,24},{5,1},{9,5},{13... | collective-permute-start | bytes 393224 | tf_op jit(solution)/shard_map/ppermute | solution.py:210
  9.8 5.3 %collective-permute-start = (bf16[128,512]{1,0:T(8,128)(2,1)}, bf16[128,512]{1,0:T(8,128)(2,1)S(1)}, u32[]{:S(2)}, u32[]{:S(2)}) collective-permute-start(bf16[128,512]{1,0:T(8,128)(2,1)} %bitcast.35), channel_id=1, source_target_pairs={{0,4},{4,8},{8,12},{12,16},{16,20},{20,24},{24,28},{1,5},{5,9},{9,... | collective-permute-start | bytes 393224 | tf_op jit(solution)/shard_map/ppermute | solution.py:209
  86.7 35.6 %collective-permute-start.3 = (bf16[27,128,512]{2,1,0:T(8,128)(2,1)}, bf16[27,128,512]{2,1,0:T(8,128)(2,1)S(1)}, u32[]{:S(2)}, u32[]{:S(2)}) collective-permute-start(bf16[27,128,512]{2,1,0:T(8,128)(2,1)} %get-tuple-element.12.mine_ref), channel_id=1, source_target_pairs={{0,4},{4,0},{8,12},{12,8},{16,20},{20,16},{24,28},{28,24},{1,5},{5... | collective-permute-start | bytes 10616840 | tf_op jit(solution)/shard_map/ppermute | solution.py:254
  104.6 8.3 %collective-permute-start.2 = (bf16[3,512,512]{2,1,0:T(8,128)(2,1)}, bf16[3,512,512]{2,1,0:T(8,128)(2,1)}, u32[]{:S(2)}, u32[]{:S(2)}) collective-permute-start(bf16[3,512,512]{2,1,0:T(8,128)(2,1)} %get-tuple-element.10), channel_id=1, source_target_pairs={{0,4},{4,0},{8,12},{12,8},{16,20},{20,16},{24,28},{28,24},{1,5},{5... | collective-permute-start | bytes 4718600 | tf_op jit(solution)/shard_map/ppermute | solution.py:253
  122.3 1.8 copy-start
Sparse Core Ops, SparseCore 0:
  24.8 62.5 reduce-scatter.1

commit v3 on v2

--- a/solution.py
+++ b/solution.py
@@ -165,19 +165,15 @@
         each_target(flipped(z, d, chan), lambda copy: copy.wait_send())
 
 
-def join_kernel(mine_ref, theirs_ref, out_ref, sems):
+def join_kernel(mine_ref, theirs_ref, out_ref):
     half = mine_ref.shape[2]
     side = lax.axis_index("vox") % 2
-    copies = [
-        pltpu.make_async_copy(
-            ref, out_ref.at[:, :, pl.ds(pl.multiple_of(place * half, half), half)], sems.at[n]
-        )
-        for n, (ref, place) in enumerate(((mine_ref, side), (theirs_ref, 1 - side)))
-    ]
-    for copy in copies:
-        copy.start()
-    for copy in copies:
-        copy.wait()
+    for place in (0, 1):
+
+        @pl.when(side == place)
+        def _():
+            out_ref[:, :, place * half : (place + 1) * half] = mine_ref[...]
+            out_ref[:, :, (1 - place) * half : (2 - place) * half] = theirs_ref[...]
 
 
 VMEM = pl.BlockSpec(memory_space=pltpu.VMEM)
@@ -259,13 +255,14 @@
     outputs = call(fold_kernel, (rows, PLANE), jnp.bfloat16, 9 * rows * PLANE * 8, 10 * rows * PLANE * 4, 32 << 20)(parts)
     outputs = outputs.reshape(rows, 1, PLANE)
 
-    anywhere = pl.BlockSpec(memory_space=pl.ANY)
+    part_spec = pl.BlockSpec((3, rows, half), lambda n: (n, 0, 0))
     weight_grad = pl.pallas_call(
         join_kernel,
+        grid=(9,),
         out_shape=jax.ShapeDtypeStruct((27, rows, cin), jnp.bfloat16),
-        in_specs=[anywhere, anywhere],
-        out_specs=anywhere,
-        scratch_shapes=[dma((2,))],
+        in_specs=[part_spec, part_spec],
+        out_specs=pl.BlockSpec((3, rows, cin), lambda n: (n, 0, 0)),
+        compiler_params=pltpu.CompilerParams(vmem_limit_bytes=32 << 20),
         cost_estimate=pl.CostEstimate(flops=0, bytes_accessed=4 * 27 * rows * cin, transcendentals=0),
     )(mine, theirs)
     return outputs, input_grad, weight_grad.transpose(1, 0, 2)

time: 349 us -> 136 us (0.39)
  Pallas kernels: 280 us -> 69.1 us
    pallas_call x1, Pallas kernels: 216 us -> 4.69 us  [local(): pl.pallas_call(join_kernel, grid=(9,), out_shape=jax.ShapeDtypeStruct((27...]
  transfers between devices with their start and end apart: 5 -> 5, of which waited for: 3 -> 3; matrix products, arithmetic and copies ran while one was open for 2% -> 6% of each run, Pallas kernels for 80% -> 50%
where the time goes in v3:
time: 136 us
  Pallas kernels  69.1 us (51%)
  starting transfers between devices  23.5 us (17%)
  between operations  14.1 us (10%)
  matrix products  13.8 us (10%)
  waiting for transfers between devices  10.5 us (8%)
  other arithmetic  4.1 us (3%)
    pallas_call x1, Pallas kernels, local(): pl.pallas_call(lambda *refs: wgrad_kernel(scale, vox, chan, *refs), out_s...  62 us
    ppermute x1, starting transfers between devices, local(): theirs = lax.ppermute(mine, 'vox', pairs)  17.8 us
    ppermute x1, waiting for transfers between devices, local(): rest = lax.ppermute(passed, 'vox', pairs)  8.23 us
    dot_general x1, matrix products, local(): jnp.einsum('okc,kov->cv', weights, back.reshape(27, rows, PLANE), preferr...  7.59 us
    dot_general x1, matrix products, local(): jnp.einsum('oabi,aip->bop', weights.reshape(rows, 3, 9, cin), full, prefe...  6.19 us
    pallas_call x1, Pallas kernels, local(): pl.pallas_call(join_kernel, grid=(9,), out_shape=jax.ShapeDtypeStruct((27...  4.69 us
    ppermute x1, starting transfers between devices, local(): below = lax.ppermute(up, 'vox', [(i, i + 1) for i in range(vox - 1)])  3.02 us
  transfers between devices with their start and end apart: 5, of which 3 were waited for; matrix products, arithmetic and copies ran while one was open for 6% of the time, Pallas kernels for 50%

profile of v3, /device:TPU:21, one launch (start us, length us, event | category | flops | bytes accessed | tf_op | source)
XLA Modules:
  0.0 135.9 jit_solution(923367276704864780)
XLA Ops:
  7.2 0.0 reduce-scatter.2.cloned.1.call-start
  7.2 2.6 %collective-permute-start.1 = (bf16[128,512]{1,0:T(8,128)(2,1)}, bf16[128,512]{1,0:T(8,128)(2,1)S(1)}, u32[]{:S(2)}, u32[]{:S(2)}) collective-permute-start(bf16[128,512]{1,0:T(8,128)(2,1)} %bitcast.34), channel_id=1, source_target_pairs={{4,0},{8,4},{12,8},{16,12},{20,16},{24,20},{28,24},{5,1},{9,5},{13... | collective-permute-start | bytes 393224 | tf_op jit(solution)/shard_map/ppermute | solution.py:206
  9.8 3.0 %collective-permute-start = (bf16[128,512]{1,0:T(8,128)(2,1)}, bf16[128,512]{1,0:T(8,128)(2,1)S(1)}, u32[]{:S(2)}, u32[]{:S(2)}) collective-permute-start(bf16[128,512]{1,0:T(8,128)(2,1)} %bitcast.35), channel_id=1, source_target_pairs={{0,4},{4,8},{8,12},{12,16},{16,20},{20,24},{24,28},{1,5},{5,9},{9,... | collective-permute-start | bytes 393224 | tf_op jit(solution)/shard_map/ppermute | solution.py:205
  12.8 0.9 collective-permute-done.1
  13.7 1.3 collective-permute-done
  15.1 0.9 pad_maximum_fusion.up_ref
  16.0 1.0 shard_map.58
  17.1 7.6 %convolution_bitcast_fusion = f32[1024,512]{0,1:T(8,128)} fusion(bf16[27,128,512]{2,1,0:T(8,128)(2,1)S(1)} %bitcast.31, bf16[128,27,1024]{2,0,1:T(8,128)(2,1)} %param.5), kind=kOutput, calls=%fused_computation.6 | convolution fusion | flops 3623878656 | bytes 12713984 | tf_op jit(solution)/shard_map/okc,kov->cv/dot_general | solution.py:209
  24.7 0.0 reduce-scatter.2.cloned.1.call-update
  24.7 62.0 %shard_map.59 = (bf16[27,128,512]{2,1,0:T(8,128)(2,1)}, bf16[3,512,512]{2,1,0:T(8,128)(2,1)}, bf16[3,512,512]{2,1,0:T(8,128)(2,1)}) custom-call(bf16[256,512]{1,0:T(8,128)(2,1)} %bitcast.41, bf16[128,512]{1,0:T(8,128)(2,1)} %bitcast.37), custom_call_target="tpu_custom_call" | custom-call | flops 28991029248 | bytes 7077888 | tf_op jit(solution)/shard_map/pallas_call | solution.py:217
  86.7 17.8 %collective-permute-start.3 = (bf16[27,128,512]{2,1,0:T(8,128)(2,1)}, bf16[27,128,512]{2,1,0:T(8,128)(2,1)S(1)}, u32[]{:S(2)}, u32[]{:S(2)}) collective-permute-start(bf16[27,128,512]{2,1,0:T(8,128)(2,1)} %get-tuple-element.12.mine_ref), channel_id=1, source_target_pairs={{0,4},{4,0},{8,12},{12,8},{16,20},{20,16},{24,28},{28,24},{1,5},{5... | collective-permute-start | bytes 10616840 | tf_op jit(solution)/shard_map/ppermute | solution.py:250
  104.5 0.1 collective-permute-start.2
  104.6 8.2 %collective-permute-done.2 = bf16[3,512,512]{2,1,0:T(8,128)(2,1)} collective-permute-done((bf16[3,512,512]{2,1,0:T(8,128)(2,1)}, bf16[3,512,512]{2,1,0:T(8,128)(2,1)}, u32[]{:S(2)}, u32[]{:S(2)}) %collective-permute-start.2) | collective-permute-done | bytes 1572896 | tf_op jit(solution)/shard_map/ppermute | solution.py:249
  112.8 2.1 %broadcast_select_fusion.1 = (bf16[3,512,512]{2,1,0:T(8,128)(2,1)S(1)}, bf16[3,512,512]{2,1,0:T(8,128)(2,1)S(1)}) fusion(bf16[3,512,512]{2,1,0:T(8,128)(2,1)} %get-tuple-element.9, bf16[3,512,512]{2,1,0:T(8,128)(2,1)} %collective-permute-done.2, pred[]{:T(512)S(6)} %eq.5), kind=kLoop, calls=%fused_computation.8 | loop fusion | flops 1572864 | bytes 6291457 | tf_op jit(solution)/shard_map/jit(_where)/select_n | solution.py:251
  114.9 0.0 copy-start
  114.9 6.2 %fusion.5.z_ref = f32[9,128,512]{2,1,0:T(8,128)S(1)} fusion(bf16[128,3,9,1024]{3,0,2,1:T(8,128)(2,1)} %bitcast.40, bf16[3,512,512]{2,1,0:T(8,128)(2,1)S(1)} %get-tuple-element.17, bf16[3,512,512]{2,1,0:T(8,128)(2,1)S(1)} %get-tuple-element.16), kind=kOutput, calls=%fused_computation.5 | convolution fusion | flops 3630170112 | bytes 12582912 | tf_op jit(solution)/shard_map/oabi,aip->bop/dot_general | solution.py:252
  121.1 1.3 shard_map.60
  122.4 0.0 collective-permute-done.3.theirs_ref
  122.4 0.0 copy-done
  122.4 4.7 %shard_map.61 = bf16[27,128,1024]{2,1,0:T(8,128)(2,1)} custom-call(bf16[27,128,512]{2,1,0:T(8,128)(2,1)S(1)} %copy-done, bf16[27,128,512]{2,1,0:T(8,128)(2,1)S(1)} %collective-permute-done.3.theirs_ref), custom_call_target="tpu_custom_call" | custom-call | bytes 14155776 | tf_op jit(solution)/shard_map/pallas_call | solution.py:259
  127.1 0.0 reduce-scatter.2.cloned.1.call-done
  127.1 1.1 convert_bitcast_fusion
  128.2 0.8 copy.10
Async XLA Ops:
  7.2 120.0 %reduce-scatter.2.cloned.1.call-start = ((), (), s32[]{:S(2)}) async-start(), calls=%async_computation.1 | async-start | bytes 2621440 | tf_op jit(solution)/shard_map/reduce_scatter | solution.py:213
  7.2 6.5 %collective-permute-start.1 = (bf16[128,512]{1,0:T(8,128)(2,1)}, bf16[128,512]{1,0:T(8,128)(2,1)S(1)}, u32[]{:S(2)}, u32[]{:S(2)}) collective-permute-start(bf16[128,512]{1,0:T(8,128)(2,1)} %bitcast.34), channel_id=1, source_target_pairs={{4,0},{8,4},{12,8},{16,12},{20,16},{24,20},{28,24},{5,1},{9,5},{13... | collective-permute-start | bytes 393224 | tf_op jit(solution)/shard_map/ppermute | solution.py:206
  9.8 5.3 %collective-permute-start = (bf16[128,512]{1,0:T(8,128)(2,1)}, bf16[128,512]{1,0:T(8,128)(2,1)S(1)}, u32[]{:S(2)}, u32[]{:S(2)}) collective-permute-start(bf16[128,512]{1,0:T(8,128)(2,1)} %bitcast.35), channel_id=1, source_target_pairs={{0,4},{4,8},{8,12},{12,16},{16,20},{20,24},{24,28},{1,5},{5,9},{9,... | collective-permute-start | bytes 393224 | tf_op jit(solution)/shard_map/ppermute | solution.py:205
  86.7 35.7 %collective-permute-start.3 = (bf16[27,128,512]{2,1,0:T(8,128)(2,1)}, bf16[27,128,512]{2,1,0:T(8,128)(2,1)S(1)}, u32[]{:S(2)}, u32[]{:S(2)}) collective-permute-start(bf16[27,128,512]{2,1,0:T(8,128)(2,1)} %get-tuple-element.12.mine_ref), channel_id=1, source_target_pairs={{0,4},{4,0},{8,12},{12,8},{16,20},{20,16},{24,28},{28,24},{1,5},{5... | collective-permute-start | bytes 10616840 | tf_op jit(solution)/shard_map/ppermute | solution.py:250
  104.5 8.3 %collective-permute-start.2 = (bf16[3,512,512]{2,1,0:T(8,128)(2,1)}, bf16[3,512,512]{2,1,0:T(8,128)(2,1)}, u32[]{:S(2)}, u32[]{:S(2)}) collective-permute-start(bf16[3,512,512]{2,1,0:T(8,128)(2,1)} %get-tuple-element.10), channel_id=1, source_target_pairs={{0,4},{4,0},{8,12},{12,8},{16,20},{20,16},{24,28},{28,24},{1,5},{5... | collective-permute-start | bytes 4718600 | tf_op jit(solution)/shard_map/ppermute | solution.py:249
  114.9 7.5 %copy-start = (bf16[27,128,512]{2,1,0:T(8,128)(2,1)S(1)}, bf16[27,128,512]{2,1,0:T(8,128)(2,1)}, u32[]{:S(2)}) copy-start(bf16[27,128,512]{2,1,0:T(8,128)(2,1)} %get-tuple-element.12.mine_ref) | copy-start | bytes 10616836
Sparse Core Ops, SparseCore 0:
  24.8 62.5 reduce-scatter.1
